TPU v7x, 128 devices: a whole 4x4x4 slice. The times are simulated.
128 devices in a mesh: rep: 16 (over x_lo, z, core), shard: 8 (over x_hi, y).
Axes of the slice: x: 4 (x_hi: 2, x_lo: 2; x = x_hi * 2 + x_lo), y: 4, z: 4, core: 2. Of those that a mesh axis runs over, the one named last changes fastest.
Arguments:
- latents: bfloat16 [16, 1024, 1024], P('rep', 'shard'), may hold values from -6 to 6
- cond: bfloat16 [16, 1024], P('rep'), may hold values from -6 to 6
- cotangent: bfloat16 [16, 1024, 1024], P('rep', 'shard'), may hold values from -6 to 6
- w_qkv: bfloat16 [1024, 3072], P('shard'), may hold values from -0.1875 to 0.1875
- bias_qv: bfloat16 [2048], P('shard'), may hold values from -3 to 3
- w_proj: bfloat16 [1024, 1024], P('shard'), may hold values from -1 to 1
- b_proj: bfloat16 [1024], P('shard'), may hold values from -3 to 3
- w_fc1: bfloat16 [1024, 4096], P('shard'), may hold values from -0.1875 to 0.1875
- b_fc1: bfloat16 [4096], P('shard'), may hold values from -3 to 3
- w_fc2: bfloat16 [4096, 1024], P('shard'), may hold values from -0.09375 to 0.09375
- b_fc2: bfloat16 [1024], P('shard'), may hold values from -3 to 3
- w_ada: bfloat16 [1024, 6144], P('shard'), may hold values from -0.1875 to 0.1875
- b_ada: bfloat16 [6144], P('shard'), may hold values from -3 to 3
Outputs:
- output: bfloat16 [16, 1024, 1024], P('rep', 'shard')
- grad_latents: bfloat16 [16, 1024, 1024], P('rep', 'shard')
- grad_cond: float32 [16, 1024], P('rep')
- grad_w_qkv: float32 [1024, 3072], P('shard')
- grad_bias_qv: float32 [2048], P('shard')
- grad_w_proj: float32 [1024, 1024], P('shard')
- grad_b_proj: float32 [1024], P('shard')
- grad_w_fc1: float32 [1024, 4096], P('shard')
- grad_b_fc1: float32 [4096], P('shard')
- grad_w_fc2: float32 [4096, 1024], P('shard')
- grad_b_fc2: float32 [1024], P('shard')
- grad_w_ada: float32 [1024, 6144], P('shard')
- grad_b_ada: float32 [6144], P('shard')
All inputs are finite; a program needn't handle non-finite values.
Results may differ from a plain program's by a relative error of at most 0.025.
Values may be sent and summed in bfloat16 or wider, within the bound.
No kernel may reach another device: no remote copies, remote signals or barrier semaphores. Data moves between devices by JAX's collectives and lax.ppermute only.
A program may use at most 192 MiB of HBM per device.

v0:
```python
import jax
import jax.numpy as jnp
from jax import lax
from jax.sharding import Mesh, PartitionSpec as P

HEAD = 64
SHARD = ("xh", "y")
CHIPS = ("xl", "z")
REP = ("xl", "z", "core")
OFFSETS = ((0, 0), (0, 1), (0, 3), (0, 2), (1, 0), (1, 1), (1, 3), (1, 2))
epsilon = 1e-06
highest = lax.Precision.HIGHEST
low = jnp.bfloat16
wide = jnp.float32


def shift(value, dx, dy):
    pairs = [(x * 4 + y, (x + dx) % 2 * 4 + (y + dy) % 4) for x in range(2) for y in range(4)]
    return lax.ppermute(value, SHARD, pairs)


def gather_turned(value):
    return [value] + [shift(value, dx, dy) for dx, dy in OFFSETS[1:]]


def scatter_turned(parts):
    total = parts[0]
    for part, (dx, dy) in zip(parts[1:], OFFSETS[1:]):
        total = total + shift(part.astype(low), dx, (4 - dy) % 4).astype(wide)
    return total


def swap_core(value):
    return lax.ppermute(value, "core", [(0, 1), (1, 0)])


def exchange(value, axes=SHARD):
    return lax.all_to_all(value, axes, 0, 0, tiled=True)


def spread(value, axes=SHARD, count=8):
    return exchange(jnp.broadcast_to(value[None], (count,) + value.shape), axes)


def normalize(values):
    centered = values - jnp.mean(values, axis=-1, keepdims=True)
    inverse = lax.rsqrt(jnp.mean(centered * centered, axis=-1, keepdims=True) + epsilon)
    return (centered * inverse, inverse)


def normalize_back(norm, inverse, grad):
    return inverse * (
        grad
        - jnp.mean(grad, axis=-1, keepdims=True)
        - norm * jnp.mean(grad * norm, axis=-1, keepdims=True)
    )


def silu(values):
    return values / (1.0 + jnp.exp(-values))


def gelu_tanh(values):
    return (
        0.5
        * values
        * (1.0 + jnp.tanh(0.7978845608028654 * (values + 0.044715 * values * values * values)))
    )


def mul(left, right):
    return lax.dot_general(left, right, (((1,), (0,)), ((), ())), preferred_element_type=wide)


def mul_t(left, right):
    return lax.dot_general(left, right, (((1,), (1,)), ((), ())), preferred_element_type=wide)


def t_mul(left, right):
    return lax.dot_general(left, right, (((0,), (0,)), ((), ())), preferred_element_type=wide)


def core_half(value, core):
    half = value.shape[0] // 2
    keep = lax.dynamic_slice_in_dim(value, core * half, half, 0)
    give = lax.dynamic_slice_in_dim(value, (1 - core) * half, half, 0).astype(low)
    return keep + swap_core(give).astype(wide)


def core_join(value, core):
    other = swap_core(value)
    first = jnp.where(core == 0, value, other)
    second = jnp.where(core == 0, other, value)
    return jnp.concatenate([first, second], axis=0)


def on_device(
    latents,
    cond,
    cotangent,
    w_qkv,
    bias_qv,
    w_proj,
    b_proj,
    w_fc1,
    b_fc1,
    w_fc2,
    b_fc2,
    w_ada,
    b_ada,
):
    stream_low = latents[0]
    upstream_low = cotangent[0]
    rows, features = stream_low.shape
    shards = 8
    own = features // shards
    units = w_fc2.shape[0]
    heads = own // HEAD
    place = lax.axis_index(SHARD)
    core = lax.axis_index("core")
    score_scale = HEAD ** (-0.5)
    cond_value = cond.astype(wide)
    cond_silu, silu_pull = jax.vjp(silu, cond_value)
    cond_low = cond_silu.astype(low)
    cond_own = lax.dynamic_slice_in_dim(cond_low, place * own, own, 1)
    mod_part = mul(cond_own, w_ada)[0]
    ada_width = w_ada.shape[1]
    blocks = jnp.arange(shards)[:, None] == place
    mod_part = mod_part + jnp.where(blocks, b_ada.astype(wide)[None, :], 0.0).reshape(ada_width)
    small = jnp.concatenate(
        [mod_part, bias_qv.astype(wide), b_proj.astype(wide), b_fc2.astype(wide)]
    )
    small_all = spread(small)
    modulation = jnp.sum(small_all[:, :ada_width], axis=0)
    shift_first, scale_first, gate_first, shift_second, scale_second, gate_second = jnp.split(
        modulation[None, :], 6, axis=1
    )
    at = ada_width
    bias_wide = small_all[:, at : at + 2 * own].reshape(1, 2 * features)
    at += 2 * own
    proj_bias = small_all[:, at : at + own].reshape(1, features)
    at += own
    second_bias = small_all[:, at : at + own].reshape(1, features)
    tokens = spread(stream_low).reshape(shards * rows, features)
    wq = exchange(
        w_qkv.reshape(own, 3, shards, own).transpose(2, 0, 1, 3).reshape(shards, own, 3 * own)
    ).reshape(features, 3 * own)
    w1 = exchange(w_fc1.reshape(own, shards, units).transpose(1, 0, 2)).reshape(features, units)
    wp = spread(w_proj).reshape(features, features)
    upstream_all = jnp.concatenate(gather_turned(upstream_low), axis=0)
    norm_first, inverse_first = normalize(tokens.astype(wide))
    attend_in = (norm_first * (1.0 + scale_first) + shift_first).astype(low)
    packed = mul(attend_in, wq)
    query_bias = lax.dynamic_slice_in_dim(bias_wide, place * own, own, 1)
    value_bias = lax.dynamic_slice_in_dim(bias_wide, features + place * own, own, 1)
    queries = (packed[:, :own] + query_bias).astype(low)
    keyset = packed[:, own : 2 * own].astype(low)
    valueset = (packed[:, 2 * own :] + value_bias).astype(low)
    length = shards * rows

    def split(value):
        return value.reshape(length, heads, HEAD)

    query_heads, key_heads, value_heads = (split(queries), split(keyset), split(valueset))
    scores = (
        jnp.einsum("qhe,khe->hqk", query_heads, key_heads, preferred_element_type=wide)
        * score_scale
    )
    row_peak = jnp.max(scores, axis=-1, keepdims=True)
    powered = jnp.exp(scores - row_peak)
    row_total = jnp.sum(powered, axis=-1, keepdims=True)
    attention = powered / row_total
    log_total = row_peak + jnp.log(row_total)
    mixed = (
        jnp.einsum("hqk,khe->qhe", attention.astype(low), value_heads, preferred_element_type=wide)
        .reshape(length, own)
        .astype(low)
    )
    mixed_tok = exchange(mixed.reshape(shards, rows, own))
    mixed_tok = mixed_tok.transpose(1, 0, 2).reshape(rows, features)
    branch = mul(mixed_tok, wp) + proj_bias
    stream = stream_low.astype(wide)
    middle = stream + gate_first * branch
    norm_second, inverse_second = normalize(middle)
    feed_in = (norm_second * (1.0 + scale_second) + shift_second).astype(low)
    feed_all = jnp.concatenate(gather_turned(feed_in), axis=0)
    hidden = mul(feed_all, w1) + b_fc1.astype(wide)[None, :]
    active_value, gelu_pull = jax.vjp(gelu_tanh, hidden)
    active = active_value.astype(low)
    branch_second_part = mul(active, w_fc2)

    def turned_parts(value):
        return [value[k * rows : (k + 1) * rows] for k in range(shards)]

    grad_branch_second = (upstream_all.astype(wide) * gate_second).astype(low)
    grad_active = mul_t(grad_branch_second, w_fc2)
    grad_hidden = gelu_pull(grad_active)[0].astype(low)
    grad_feed = scatter_turned(turned_parts(mul_t(grad_hidden, w1)))
    branch_second = scatter_turned(turned_parts(branch_second_part)) + second_bias
    output = (middle + gate_second * branch_second).astype(low)
    upstream = upstream_low.astype(wide)
    grad_gate_second = jnp.sum(upstream * branch_second, axis=0)
    grad_scale_second = jnp.sum(grad_feed * norm_second, axis=0)
    grad_shift_second = jnp.sum(grad_feed, axis=0)
    grad_middle = upstream + normalize_back(
        norm_second, inverse_second, grad_feed * (1.0 + scale_second)
    )
    grad_gate_first = jnp.sum(grad_middle * branch, axis=0)
    grad_branch = (grad_middle * gate_first).astype(low)
    grad_mixed_tok = mul_t(grad_branch, wp).astype(low)
    grad_mixed = exchange(grad_mixed_tok.reshape(rows, shards, own).transpose(1, 0, 2))
    grad_mixed = split(grad_mixed.reshape(length, own))
    again_scores = (
        jnp.einsum("qhe,khe->hqk", query_heads, key_heads, preferred_element_type=wide)
        * score_scale
    )
    again = jnp.exp(again_scores - log_total)
    grad_probs = jnp.einsum("qhe,khe->hqk", grad_mixed, value_heads, preferred_element_type=wide)
    grad_value = jnp.einsum(
        "hqk,qhe->khe", again.astype(low), grad_mixed, preferred_element_type=wide
    )
    row_delta = jnp.sum(again * grad_probs, axis=-1, keepdims=True)
    grad_scores = (again * (grad_probs - row_delta)).astype(low)
    grad_query = (
        jnp.einsum("hqk,khe->qhe", grad_scores, key_heads, preferred_element_type=wide)
        * score_scale
    )
    grad_key = (
        jnp.einsum("hqk,qhe->khe", grad_scores, query_heads, preferred_element_type=wide)
        * score_scale
    )
    grad_packed = jnp.concatenate(
        [part.reshape(length, own).astype(low) for part in (grad_query, grad_key, grad_value)],
        axis=1,
    )
    attend_part = mul_t(grad_packed, wq)
    grad_scale_first = jnp.sum(attend_part * norm_first, axis=0)
    grad_shift_first = jnp.sum(attend_part, axis=0)
    attend_sent = exchange(attend_part.astype(low).reshape(shards, rows, features))
    grad_attend = jnp.sum(attend_sent.astype(wide), axis=0)
    norm_own, inverse_own = normalize(stream)
    grad_stream = grad_middle + normalize_back(
        norm_own, inverse_own, grad_attend * (1.0 + scale_first)
    )
    grad_latents = grad_stream.astype(low)
    mod_terms = jnp.concatenate(
        [
            grad_shift_first,
            grad_scale_first,
            grad_gate_first,
            grad_shift_second,
            grad_scale_second,
            grad_gate_second,
            jnp.sum(grad_branch.astype(wide), axis=0),
        ]
    )
    mod_sums = jnp.sum(spread(mod_terms), axis=0)
    grad_modulation = mod_sums[:ada_width]
    proj_bias_term = lax.dynamic_slice_in_dim(mod_sums, ada_width + place * own, own, 0)
    cond_term = jnp.sum(w_ada.astype(wide) * grad_modulation[None, :], axis=1)
    cond_total = spread(cond_term).reshape(1, features)
    grad_cond = silu_pull(cond_total)[0]
    packed_sums = jnp.sum(grad_packed.astype(wide), axis=0)
    second_bias_sums = jnp.sum(grad_branch_second.astype(wide), axis=0)
    rep_terms = jnp.concatenate(
        [
            grad_modulation,
            cond_own[0].astype(wide),
            proj_bias_term,
            jnp.sum(grad_hidden.astype(wide), axis=0),
            lax.dynamic_slice_in_dim(second_bias_sums, place * own, own, 0),
            packed_sums,
        ]
    )
    rep_all = spread(rep_terms, REP, 16)
    grad_w_ada = lax.dot_general(
        rep_all[:, ada_width : ada_width + own],
        rep_all[:, :ada_width],
        (((0,), (0,)), ((), ())),
        precision=highest,
        preferred_element_type=wide,
    )
    rep_sums = jnp.sum(rep_all, axis=0)
    ada_own = ada_width // shards
    grad_b_ada = lax.dynamic_slice_in_dim(rep_sums, place * ada_own, ada_own, 0)
    at = ada_width + own
    grad_b_proj = rep_sums[at : at + own]
    at += own
    grad_b_fc1 = rep_sums[at : at + units]
    at += units
    grad_b_fc2 = rep_sums[at : at + own]
    at += own
    bias_all = spread(jnp.concatenate([rep_sums[at : at + own], rep_sums[at + 2 * own :]]))
    bias_all = jnp.concatenate(
        [bias_all[:, :own].reshape(features), bias_all[:, own:].reshape(features)]
    )
    grad_bias_qv = lax.dynamic_slice_in_dim(bias_all, place * 2 * own, 2 * own, 0)

    def over_rep(value):
        owned = lax.psum_scatter(value.astype(low), CHIPS, scatter_dimension=0, tiled=True)
        return core_join(lax.all_gather(owned, CHIPS, axis=0, tiled=True), core).astype(wide)

    term_second = core_half(t_mul(active, grad_branch_second), core)
    grad_w_fc2 = over_rep(term_second)
    term_first = core_half(
        t_mul(feed_all, grad_hidden)
        .reshape(shards, own, units)
        .transpose(1, 0, 2)
        .reshape(own, shards * units),
        core,
    )
    term_first = exchange(
        term_first.astype(low).reshape(own // 2, shards, units).transpose(1, 0, 2)
    )
    term_first = term_first.transpose(1, 0, 2).reshape(own // 2, shards * units)
    grad_w_fc1 = over_rep(term_first)
    term_proj = t_mul(mixed_tok, grad_branch).reshape(shards, own, features)
    term_proj = core_half(term_proj.transpose(1, 0, 2), core)
    term_proj = exchange(term_proj.astype(low).transpose(1, 0, 2))
    grad_w_proj = over_rep(jnp.sum(term_proj.astype(wide), axis=0))
    term_qkv = t_mul(attend_in, grad_packed).reshape(shards, own, 3 * own)
    term_qkv = core_half(term_qkv.transpose(1, 0, 2), core)
    term_qkv = exchange(term_qkv.astype(low).transpose(1, 0, 2))
    term_qkv = (
        term_qkv.reshape(shards, own // 2, 3, own)
        .transpose(1, 2, 0, 3)
        .reshape(own // 2, 3 * features)
    )
    grad_w_qkv = over_rep(term_qkv)
    return (
        output[None],
        grad_latents[None],
        grad_cond,
        grad_w_qkv,
        grad_bias_qv,
        grad_w_proj,
        grad_b_proj,
        grad_w_fc1,
        grad_b_fc1,
        grad_w_fc2,
        grad_b_fc2,
        grad_w_ada,
        grad_b_ada,
    )


def solution(mesh):
    fine = Mesh(mesh.devices.reshape(2, 4, 2, 2, 4), REP + SHARD)
    tokens = P(REP, SHARD, None)
    matrix = P(SHARD, None)
    vector = P(SHARD)
    params = (matrix, vector) * 5
    return jax.shard_map(
        on_device,
        mesh=fine,
        in_specs=(tokens, P(REP, None), tokens) + params,
        out_specs=(tokens, tokens, P(REP, None)) + params,
        check_vma=False,
    )
```

profile of v0, /device:TPU:0, one launch (start us, length us, event | category | flops | bytes accessed | tf_op | source)
XLA Modules:
  0.0 621.3 jit_solution(15007044505543565158)
XLA Ops:
  14.0 7.0 %all-to-all-start = ((f32[8,1,6656]{2,1,0:T(1,128)}), f32[8,1,6656]{2,1,0:T(1,128)S(1)}, u32[]{:S(2)}, u32[]{:S(2)}) async-start(f32[8,1,6656]{2,1,0:T(1,128)} %broadcast_in_dim.43), calls=%async_computation | async-start | bytes 425984 | tf_op jit(solution)/shard_map/all_to_all | solution.py:38
  23.5 6.0 all-to-all-done
  33.1 5.6 collective-permute-start.19
  48.6 8.6 %all-to-all-start.1 = ((bf16[8,128,1024]{2,1,0:T(8,128)(2,1)}), bf16[8,128,1024]{2,1,0:T(8,128)(2,1)S(1)}, u32[]{:S(2)}, u32[]{:S(2)}) async-start(bf16[8,128,1024]{2,1,0:T(8,128)(2,1)} %broadcast_in_dim.45), calls=%async_computation.1 | async-start | bytes 4194304 | tf_op jit(solution)/shard_map/all_to_all | solution.py:38
  59.9 9.9 %collective-permute-done.14 = bf16[128,1024]{1,0:T(8,128)(2,1)} collective-permute-done((bf16[128,1024]{1,0:T(8,128)(2,1)}, bf16[128,1024]{1,0:T(8,128)(2,1)}, u32[]{:S(2)}, u32[]{:S(2)}) %collective-permute-start.14) | collective-permute-done | bytes 262176 | tf_op jit(solution)/shard_map/ppermute | solution.py:19
  69.8 8.2 %collective-permute-start.17 = (bf16[128,1024]{1,0:T(8,128)(2,1)}, bf16[128,1024]{1,0:T(8,128)(2,1)S(1)}, u32[]{:S(2)}, u32[]{:S(2)}) collective-permute-start(bf16[128,1024]{1,0:T(8,128)(2,1)} %bitcast.30), channel_id=1, source_target_pairs={{0,4},{1,5},{2,6},{3,7},{4,0},{5,1},{6,2},{7,3},{8,12},{9,13},{10,... | collective-permute-start | bytes 786440 | tf_op jit(solution)/shard_map/ppermute | solution.py:19
  109.7 10.5 %all-to-all-done.4 = bf16[8,128,1024]{2,1,0:T(8,128)(2,1)} async-done(((bf16[8,128,1024]{2,1,0:T(8,128)(2,1)}), bf16[8,128,1024]{2,1,0:T(8,128)(2,1)}, u32[]{:S(2)}, u32[]{:S(2)}) %all-to-all-start.4) | async-done | bytes 2097184 | tf_op jit(solution)/shard_map/all_to_all | solution.py:38
  120.2 4.7 all-to-all-start.3
  128.3 5.5 all-to-all-done.3
  146.3 6.5 %all-to-all-done.5 = bf16[8,128,512]{1,2,0:T(8,128)(2,1)} async-done(((bf16[8,128,512]{1,2,0:T(8,128)(2,1)}), bf16[8,128,512]{1,2,0:T(8,128)(2,1)}, u32[]{:S(2)}, u32[]{:S(2)}) %all-to-all-start.5) | async-done | bytes 1048608 | tf_op jit(solution)/shard_map/all_to_all | solution.py:38
  169.0 9.7 %collective-permute-done.1 = bf16[128,1024]{1,0:T(8,128)(2,1)} collective-permute-done((bf16[128,1024]{1,0:T(8,128)(2,1)}, bf16[128,1024]{1,0:T(8,128)(2,1)}, u32[]{:S(2)}, u32[]{:S(2)}) %collective-permute-start.1) | collective-permute-done | bytes 262176 | tf_op jit(solution)/shard_map/ppermute | solution.py:19
  178.7 5.5 collective-permute-start.4
  202.9 4.6 convert_reduce_fusion.3
  219.7 4.9 collective-permute-start.13
  227.6 4.8 collective-permute-start.26
  232.3 4.6 fusion.13
  240.3 5.3 collective-permute-start.25
  293.4 4.9 all-to-all-done.6
  298.7 5.1 fusion.16
  303.8 4.6 multiply_reduce_fusion
  337.6 11.0 %all-to-all-done.14 = bf16[8,64,512]{2,1,0:T(8,128)(2,1)S(1)} async-done(((bf16[8,64,512]{2,1,0:T(8,128)(2,1)}), bf16[8,64,512]{2,1,0:T(8,128)(2,1)S(1)}, u32[]{:S(2)}, u32[]{:S(2)}) %all-to-all-start.14) | async-done | bytes 524320 | tf_op jit(solution)/shard_map/all_to_all | solution.py:38
  355.4 6.4 %all-to-all-done.10 = bf16[8,64,384]{2,1,0:T(8,128)(2,1)S(1)} async-done(((bf16[8,64,384]{2,1,0:T(8,128)(2,1)}), bf16[8,64,384]{2,1,0:T(8,128)(2,1)S(1)}, u32[]{:S(2)}, u32[]{:S(2)}) %all-to-all-start.10) | async-done | bytes 393248 | tf_op jit(solution)/shard_map/all_to_all | solution.py:38
  366.8 12.5 %all-to-all-done.13 = bf16[8,64,1024]{2,1,0:T(8,128)(2,1)S(1)} async-done(((bf16[8,64,1024]{2,1,0:T(8,128)(2,1)}), bf16[8,64,1024]{2,1,0:T(8,128)(2,1)S(1)}, u32[]{:S(2)}, u32[]{:S(2)}) %all-to-all-start.13) | async-done | bytes 1048608 | tf_op jit(solution)/shard_map/all_to_all | solution.py:38
  387.4 51.2 %all_gather.15 = bf16[256,1024]{1,0:T(8,128)(2,1)} all-gather(bf16[32,1024]{1,0:T(8,128)(2,1)} %reduce-scatter.11.cloned.1.call-done), channel_id=1, replica_groups=mesh['xl'=2,'z'=4,'core'=2,'xh'=2,'y'=4] {'xl','z'}, dimensions={0}, use_global_device_ids=true | all-gather | bytes 589824 | tf_op jit(solution)/shard_map/all_gather | solution.py:301
  439.9 30.9 %all_gather.12 = bf16[64,3072]{1,0:T(8,128)(2,1)} all-gather(bf16[8,3072]{1,0:T(8,128)(2,1)} %reduce-scatter.5.cloned.1.call-done), channel_id=1, replica_groups=mesh['xl'=2,'z'=4,'core'=2,'xh'=2,'y'=4] {'xl','z'}, dimensions={0}, use_global_device_ids=true | all-gather | bytes 442368 | tf_op jit(solution)/shard_map/all_gather | solution.py:301
  470.8 31.3 %all_gather.14 = bf16[64,4096]{1,0:T(8,128)(2,1)} all-gather(bf16[8,4096]{1,0:T(8,128)(2,1)} %reduce-scatter.9.cloned.1.call-done), channel_id=1, replica_groups=mesh['xl'=2,'z'=4,'core'=2,'xh'=2,'y'=4] {'xl','z'}, dimensions={0}, use_global_device_ids=true | all-gather | bytes 589824 | tf_op jit(solution)/shard_map/all_gather | solution.py:301
  508.9 7.6 %all-to-all-start.8 = ((f32[8,1,7168]{2,1,0:T(1,128)}), f32[8,1,7168]{2,1,0:T(1,128)S(1)}, u32[]{:S(2)}, u32[]{:S(2)}) async-start(f32[8,1,7168]{2,1,0:T(1,128)} %broadcast_in_dim.49), calls=%async_computation.8 | async-start | bytes 458752 | tf_op jit(solution)/shard_map/all_to_all | solution.py:38
  519.1 23.9 %reduce-scatter.7.cloned.1.call-done = bf16[8,1024]{1,0:T(8,128)(2,1)} async-done(((bf16[64,1024]{1,0:T(8,128)(2,1)}), bf16[8,1024]{1,0:T(8,128)(2,1)}) %reduce-scatter.7.cloned.1.call-update) | async-done | bytes 16400 | tf_op jit(solution)/shard_map/reduce_scatter | solution.py:300
  543.0 28.4 %all_gather.13 = bf16[64,1024]{1,0:T(8,128)(2,1)S(1)} all-gather(bf16[8,1024]{1,0:T(8,128)(2,1)} %reduce-scatter.7.cloned.1.call-done), channel_id=1, replica_groups=mesh['xl'=2,'z'=4,'core'=2,'xh'=2,'y'=4] {'xl','z'}, dimensions={0}, use_global_device_ids=true | all-gather | bytes 147456 | tf_op jit(solution)/shard_map/all_gather | solution.py:301
  572.7 6.4 %all-to-all-start.9 = ((f32[8,1,128]{2,1,0:T(1,128)}), f32[8,1,128]{2,1,0:T(1,128)S(1)}, u32[]{:S(2)}, u32[]{:S(2)}) async-start(f32[8,1,128]{2,1,0:T(1,128)} %broadcast_in_dim.50), calls=%async_computation.9 | async-start | bytes 8192 | tf_op jit(solution)/shard_map/all_to_all | solution.py:38
  579.3 7.4 %all-to-all-done.9 = f32[8,1,128]{2,1,0:T(1,128)S(1)} async-done(((f32[8,1,128]{2,1,0:T(1,128)}), f32[8,1,128]{2,1,0:T(1,128)S(1)}, u32[]{:S(2)}, u32[]{:S(2)}) %all-to-all-start.9) | async-done | bytes 4128 | tf_op jit(solution)/shard_map/all_to_all | solution.py:38
  595.6 6.0 all-to-all-done.11
  (333 shorter events, 256.8 us)
Async XLA Ops:
  33.1 93.5 %collective-permute-start.19 = (bf16[128,1024]{1,0:T(8,128)(2,1)}, bf16[128,1024]{1,0:T(8,128)(2,1)}, u32[]{:S(2)}, u32[]{:S(2)}) collective-permute-start(bf16[128,1024]{1,0:T(8,128)(2,1)} %bitcast.30), channel_id=1, source_target_pairs={{0,7},{1,4},{2,5},{3,6},{4,3},{5,0},{6,1},{7,2},{8,15},{9,12},{10,... | collective-permute-start | bytes 786440 | tf_op jit(solution)/shard_map/ppermute | solution.py:19
  38.6 86.3 %collective-permute-start.18 = (bf16[128,1024]{1,0:T(8,128)(2,1)}, bf16[128,1024]{1,0:T(8,128)(2,1)}, u32[]{:S(2)}, u32[]{:S(2)}) collective-permute-start(bf16[128,1024]{1,0:T(8,128)(2,1)} %bitcast.30), channel_id=1, source_target_pairs={{0,5},{1,6},{2,7},{3,4},{4,1},{5,2},{6,3},{7,0},{8,13},{9,14},{10,... | collective-permute-start | bytes 786440 | tf_op jit(solution)/shard_map/ppermute | solution.py:19
  38.6 42.8 %collective-permute-start.16 = (bf16[128,1024]{1,0:T(8,128)(2,1)}, bf16[128,1024]{1,0:T(8,128)(2,1)}, u32[]{:S(2)}, u32[]{:S(2)}) collective-permute-start(bf16[128,1024]{1,0:T(8,128)(2,1)} %bitcast.30), channel_id=1, source_target_pairs={{0,2},{1,3},{2,0},{3,1},{4,6},{5,7},{6,4},{7,5},{8,10},{9,11},{10,... | collective-permute-start | bytes 786440 | tf_op jit(solution)/shard_map/ppermute | solution.py:19
  40.9 38.8 %collective-permute-start.15 = (bf16[128,1024]{1,0:T(8,128)(2,1)}, bf16[128,1024]{1,0:T(8,128)(2,1)}, u32[]{:S(2)}, u32[]{:S(2)}) collective-permute-start(bf16[128,1024]{1,0:T(8,128)(2,1)} %bitcast.30), channel_id=1, source_target_pairs={{0,3},{1,0},{2,1},{3,2},{4,7},{5,4},{6,5},{7,6},{8,11},{9,8},{10,9... | collective-permute-start | bytes 786440 | tf_op jit(solution)/shard_map/ppermute | solution.py:19
  42.1 27.7 %collective-permute-start.14 = (bf16[128,1024]{1,0:T(8,128)(2,1)}, bf16[128,1024]{1,0:T(8,128)(2,1)}, u32[]{:S(2)}, u32[]{:S(2)}) collective-permute-start(bf16[128,1024]{1,0:T(8,128)(2,1)} %bitcast.30), channel_id=1, source_target_pairs={{0,1},{1,2},{2,3},{3,0},{4,5},{5,6},{6,7},{7,4},{8,9},{9,10},{10,1... | collective-permute-start | bytes 786440 | tf_op jit(solution)/shard_map/ppermute | solution.py:19
  48.6 41.6 %all-to-all-start.1 = ((bf16[8,128,1024]{2,1,0:T(8,128)(2,1)}), bf16[8,128,1024]{2,1,0:T(8,128)(2,1)S(1)}, u32[]{:S(2)}, u32[]{:S(2)}) async-start(bf16[8,128,1024]{2,1,0:T(8,128)(2,1)} %broadcast_in_dim.45), calls=%async_computation.1 | async-start | bytes 4194304 | tf_op jit(solution)/shard_map/all_to_all | solution.py:38
  79.7 64.9 %collective-permute-start.20 = (bf16[128,1024]{1,0:T(8,128)(2,1)}, bf16[128,1024]{1,0:T(8,128)(2,1)}, u32[]{:S(2)}, u32[]{:S(2)}) collective-permute-start(bf16[128,1024]{1,0:T(8,128)(2,1)} %bitcast.30), channel_id=1, source_target_pairs={{0,6},{1,7},{2,4},{3,5},{4,2},{5,3},{6,0},{7,1},{8,14},{9,15},{10,... | collective-permute-start | bytes 786440 | tf_op jit(solution)/shard_map/ppermute | solution.py:19
  92.7 27.4 %all-to-all-start.4 = ((bf16[8,128,1024]{2,1,0:T(8,128)(2,1)}), bf16[8,128,1024]{2,1,0:T(8,128)(2,1)}, u32[]{:S(2)}, u32[]{:S(2)}) async-start(bf16[8,128,1024]{2,1,0:T(8,128)(2,1)} %broadcast_in_dim.46), calls=%async_computation.4 | async-start | bytes 4194304 | tf_op jit(solution)/shard_map/all_to_all | solution.py:38
  142.8 23.5 %collective-permute-start = (bf16[128,1024]{1,0:T(8,128)(2,1)}, bf16[128,1024]{1,0:T(8,128)(2,1)}, u32[]{:S(2)}, u32[]{:S(2)}) collective-permute-start(bf16[128,1024]{1,0:T(8,128)(2,1)} %get-tuple-element.28), channel_id=1, source_target_pairs={{0,1},{1,2},{2,3},{3,0},{4,5},{5,6},{6,7},{7,4},{8,9},{9,10},{10,1... | collective-permute-start | bytes 786440 | tf_op jit(solution)/shard_map/ppermute | solution.py:19
  155.1 30.8 %collective-permute-start.2 = (bf16[128,1024]{1,0:T(8,128)(2,1)}, bf16[128,1024]{1,0:T(8,128)(2,1)}, u32[]{:S(2)}, u32[]{:S(2)}) collective-permute-start(bf16[128,1024]{1,0:T(8,128)(2,1)} %get-tuple-element.28), channel_id=1, source_target_pairs={{0,2},{1,3},{2,0},{3,1},{4,6},{5,7},{6,4},{7,5},{8,10},{9,11},{10,... | collective-permute-start | bytes 786440 | tf_op jit(solution)/shard_map/ppermute | solution.py:19
  157.2 21.5 %collective-permute-start.1 = (bf16[128,1024]{1,0:T(8,128)(2,1)}, bf16[128,1024]{1,0:T(8,128)(2,1)}, u32[]{:S(2)}, u32[]{:S(2)}) collective-permute-start(bf16[128,1024]{1,0:T(8,128)(2,1)} %get-tuple-element.28), channel_id=1, source_target_pairs={{0,3},{1,0},{2,1},{3,2},{4,7},{5,4},{6,5},{7,6},{8,11},{9,8},{10,9... | collective-permute-start | bytes 786440 | tf_op jit(solution)/shard_map/ppermute | solution.py:19
  158.5 35.7 %collective-permute-start.6 = (bf16[128,1024]{1,0:T(8,128)(2,1)}, bf16[128,1024]{1,0:T(8,128)(2,1)}, u32[]{:S(2)}, u32[]{:S(2)}) collective-permute-start(bf16[128,1024]{1,0:T(8,128)(2,1)} %get-tuple-element.28), channel_id=1, source_target_pairs={{0,6},{1,7},{2,4},{3,5},{4,2},{5,3},{6,0},{7,1},{8,14},{9,15},{10,... | collective-permute-start | bytes 786440 | tf_op jit(solution)/shard_map/ppermute | solution.py:19
  161.8 30.7 %collective-permute-start.5 = (bf16[128,1024]{1,0:T(8,128)(2,1)}, bf16[128,1024]{1,0:T(8,128)(2,1)}, u32[]{:S(2)}, u32[]{:S(2)}) collective-permute-start(bf16[128,1024]{1,0:T(8,128)(2,1)} %get-tuple-element.28), channel_id=1, source_target_pairs={{0,7},{1,4},{2,5},{3,6},{4,3},{5,0},{6,1},{7,2},{8,15},{9,12},{10,... | collective-permute-start | bytes 786440 | tf_op jit(solution)/shard_map/ppermute | solution.py:19
  166.2 21.3 %collective-permute-start.3 = (bf16[128,1024]{1,0:T(8,128)(2,1)}, bf16[128,1024]{1,0:T(8,128)(2,1)S(1)}, u32[]{:S(2)}, u32[]{:S(2)}) collective-permute-start(bf16[128,1024]{1,0:T(8,128)(2,1)} %get-tuple-element.28), channel_id=1, source_target_pairs={{0,4},{1,5},{2,6},{3,7},{4,0},{5,1},{6,2},{7,3},{8,12},{9,13},{10,... | collective-permute-start | bytes 786440 | tf_op jit(solution)/shard_map/ppermute | solution.py:19
  219.7 20.6 %collective-permute-start.7 = (bf16[128,1024]{1,0:T(8,128)(2,1)S(1)}, bf16[128,1024]{1,0:T(8,128)(2,1)S(1)}, u32[]{:S(2)}, u32[]{:S(2)}) collective-permute-start(bf16[128,1024]{1,0:T(8,128)(2,1)S(1)} %get-tuple-element.40), channel_id=1, source_target_pairs={{0,3},{1,0},{2,1},{3,2},{4,7},{5,4},{6,5},{7,6},{8,11},{9,8},{10,9... | collective-permute-start | bytes 786440 | tf_op jit(solution)/shard_map/ppermute | solution.py:19
  219.7 25.9 %collective-permute-start.13 = (bf16[128,1024]{1,0:T(8,128)(2,1)S(1)}, bf16[128,1024]{1,0:T(8,128)(2,1)S(1)}, u32[]{:S(2)}, u32[]{:S(2)}) collective-permute-start(bf16[128,1024]{1,0:T(8,128)(2,1)S(1)} %get-tuple-element.41), channel_id=1, source_target_pairs={{0,6},{1,7},{2,4},{3,5},{4,2},{5,3},{6,0},{7,1},{8,14},{9,15},{10,... | collective-permute-start | bytes 786440 | tf_op jit(solution)/shard_map/ppermute | solution.py:19
  225.8 21.9 %collective-permute-start.21 = (bf16[128,1024]{1,0:T(8,128)(2,1)S(1)}, bf16[128,1024]{1,0:T(8,128)(2,1)S(1)}, u32[]{:S(2)}, u32[]{:S(2)}) collective-permute-start(bf16[128,1024]{1,0:T(8,128)(2,1)S(1)} %get-tuple-element.33), channel_id=1, source_target_pairs={{0,3},{1,0},{2,1},{3,2},{4,7},{5,4},{6,5},{7,6},{8,11},{9,8},{10,9... | collective-permute-start | bytes 786440 | tf_op jit(solution)/shard_map/ppermute | solution.py:19
  227.2 20.7 %collective-permute-start.27 = (bf16[128,1024]{1,0:T(8,128)(2,1)S(1)}, bf16[128,1024]{1,0:T(8,128)(2,1)S(1)}, u32[]{:S(2)}, u32[]{:S(2)}) collective-permute-start(bf16[128,1024]{1,0:T(8,128)(2,1)S(1)} %get-tuple-element.34), channel_id=1, source_target_pairs={{0,6},{1,7},{2,4},{3,5},{4,2},{5,3},{6,0},{7,1},{8,14},{9,15},{10,... | collective-permute-start | bytes 786440 | tf_op jit(solution)/shard_map/ppermute | solution.py:19
  227.6 28.5 %collective-permute-start.26 = (bf16[128,1024]{1,0:T(8,128)(2,1)}, bf16[128,1024]{1,0:T(8,128)(2,1)}, u32[]{:S(2)}, u32[]{:S(2)}) collective-permute-start(bf16[128,1024]{1,0:T(8,128)(2,1)} %get-tuple-element.35), channel_id=1, source_target_pairs={{0,5},{1,6},{2,7},{3,4},{4,1},{5,2},{6,3},{7,0},{8,13},{9,14},{10,... | collective-permute-start | bytes 786440 | tf_op jit(solution)/shard_map/ppermute | solution.py:19
  269.3 55.2 %collective-permute-start.34 = (bf16[256,1024]{1,0:T(8,128)(2,1)}, bf16[256,1024]{1,0:T(8,128)(2,1)}, u32[]{:S(2)}, u32[]{:S(2)}) collective-permute-start(bf16[256,1024]{1,0:T(8,128)(2,1)} %dynamic-slice_convert_fusion.1), channel_id=1, source_target_pairs={{0,8},{8,0},{1,9},{9,1},{2,10},{10,2},{3,11},{11,3},{4,12},{12,4},... | collective-permute-start | bytes 1572872 | tf_op jit(solution)/shard_map/ppermute | solution.py:34
  273.9 52.8 %collective-permute-start.32 = (bf16[64,4096]{1,0:T(8,128)(2,1)}, bf16[64,4096]{1,0:T(8,128)(2,1)}, u32[]{:S(2)}, u32[]{:S(2)}) collective-permute-start(bf16[64,4096]{1,0:T(8,128)(2,1)} %copy.202), channel_id=1, source_target_pairs={{0,8},{8,0},{1,9},{9,1},{2,10},{10,2},{3,11},{11,3},{4,12},{12,4},... | collective-permute-start | bytes 1572872 | tf_op jit(solution)/shard_map/ppermute | solution.py:34
  289.2 98.2 %reduce-scatter.11.cloned.1.call-start = ((), (), s32[]{:S(2)}) async-start(), calls=%async_computation.22 | async-start | bytes 589824 | tf_op jit(solution)/shard_map/reduce_scatter | solution.py:300
  293.2 58.9 %collective-permute-start.30 = (bf16[64,8,1024]{2,0,1:T(8,128)(2,1)}, bf16[64,8,1024]{2,0,1:T(8,128)(2,1)}, u32[]{:S(2)}, u32[]{:S(2)}) collective-permute-start(bf16[64,8,1024]{2,0,1:T(8,128)(2,1)} %fusion.23), channel_id=1, source_target_pairs={{0,8},{8,0},{1,9},{9,1},{2,10},{10,2},{3,11},{11,3},{4,12},{12,4},... | collective-permute-start | bytes 3145736 | tf_op jit(solution)/shard_map/ppermute | solution.py:34
  365.3 74.6 %reduce-scatter.5.cloned.1.call-start = ((), (), s32[]{:S(2)}) async-start(), calls=%async_computation.19 | async-start | bytes 442368 | tf_op jit(solution)/shard_map/reduce_scatter | solution.py:300
  379.3 126.6 %all-to-all-start.7 = ((bf16[8,128,1024]{2,1,0:T(8,128)(2,1)}), bf16[8,128,1024]{2,1,0:T(8,128)(2,1)S(1)}, u32[]{:S(2)}, u32[]{:S(2)}) async-start(bf16[8,128,1024]{2,1,0:T(8,128)(2,1)} %bitcast.216), calls=%async_computation.7 | async-start | bytes 4194304 | tf_op jit(solution)/shard_map/all_to_all | solution.py:38
  383.0 87.8 %reduce-scatter.9.cloned.1.call-start = ((), (), s32[]{:S(2)}) async-start(), calls=%async_computation.21 | async-start | bytes 589824 | tf_op jit(solution)/shard_map/reduce_scatter | solution.py:300
  385.0 158.0 %reduce-scatter.7.cloned.1.call-start = ((), (), s32[]{:S(2)}) async-start(), calls=%async_computation.20 | async-start | bytes 147456 | tf_op jit(solution)/shard_map/reduce_scatter | solution.py:300
  438.6 63.6 %collective-permute-start.35 = (bf16[256,1024]{1,0:T(8,128)(2,1)}, bf16[256,1024]{1,0:T(8,128)(2,1)}, u32[]{:S(2)}, u32[]{:S(2)}) collective-permute-start(bf16[256,1024]{1,0:T(8,128)(2,1)} %all_gather.15), channel_id=1, source_target_pairs={{0,8},{8,0},{1,9},{9,1},{2,10},{10,2},{3,11},{11,3},{4,12},{12,4},... | collective-permute-start | bytes 1572872 | tf_op jit(solution)/shard_map/ppermute | solution.py:34
  470.8 45.6 %collective-permute-start.29 = (bf16[64,3072]{1,0:T(8,128)(2,1)}, bf16[64,3072]{1,0:T(8,128)(2,1)}, u32[]{:S(2)}, u32[]{:S(2)}) collective-permute-start(bf16[64,3072]{1,0:T(8,128)(2,1)} %all_gather.12), channel_id=1, source_target_pairs={{0,8},{8,0},{1,9},{9,1},{2,10},{10,2},{3,11},{11,3},{4,12},{12,4},... | collective-permute-start | bytes 1179656 | tf_op jit(solution)/shard_map/ppermute | solution.py:34
  502.1 89.8 %collective-permute-start.33 = (bf16[64,4096]{1,0:T(8,128)(2,1)}, bf16[64,4096]{1,0:T(8,128)(2,1)}, u32[]{:S(2)}, u32[]{:S(2)}) collective-permute-start(bf16[64,4096]{1,0:T(8,128)(2,1)} %all_gather.14), channel_id=1, source_target_pairs={{0,8},{8,0},{1,9},{9,1},{2,10},{10,2},{3,11},{11,3},{4,12},{12,4},... | collective-permute-start | bytes 1572872 | tf_op jit(solution)/shard_map/ppermute | solution.py:34
  508.9 62.6 %all-to-all-start.8 = ((f32[8,1,7168]{2,1,0:T(1,128)}), f32[8,1,7168]{2,1,0:T(1,128)S(1)}, u32[]{:S(2)}, u32[]{:S(2)}) async-start(f32[8,1,7168]{2,1,0:T(1,128)} %broadcast_in_dim.49), calls=%async_computation.8 | async-start | bytes 458752 | tf_op jit(solution)/shard_map/all_to_all | solution.py:38
  571.4 23.3 %collective-permute-start.31 = (bf16[64,1024]{1,0:T(8,128)(2,1)S(1)}, bf16[64,1024]{1,0:T(8,128)(2,1)S(1)}, u32[]{:S(2)}, u32[]{:S(2)}) collective-permute-start(bf16[64,1024]{1,0:T(8,128)(2,1)S(1)} %all_gather.13), channel_id=1, source_target_pairs={{0,8},{8,0},{1,9},{9,1},{2,10},{10,2},{3,11},{11,3},{4,12},{12,4},... | collective-permute-start | bytes 393224 | tf_op jit(solution)/shard_map/ppermute | solution.py:34
  (68 other events, 1010.4 us)
Sparse Core Ops, SparseCore 0:
  326.8 36.9 reduce-scatter.10
  368.6 41.2 reduce-scatter.4
  412.8 36.7 reduce-scatter.8
  506.0 36.9 reduce-scatter.6
where the time goes:
time: 628 us; the launch traced here: 621 us
  waiting for transfers between devices  148 us (24%)
  blocking collectives  142 us (23%)
  starting transfers between devices  138 us (22%)
  local copies, waits for them, and re-layouts  78.6 us (13%)
  matrix products  57 us (9%)
  other arithmetic  43.1 us (7%)
  between operations  15 us (2%)
    all_gather x4, blocking collectives, over_rep(): lax.all_gather(owned, CHIPS, axis=0, tiled=True)  142 us
    all_to_all x15, waiting for transfers between devices, exchange(): return lax.all_to_all(value, axes, 0, 0, tiled=True)  81.2 us
    all_to_all x15, starting transfers between devices, exchange(): return lax.all_to_all(value, axes, 0, 0, tiled=True)  71.2 us
    ppermute x28, starting transfers between devices, shift(): return lax.ppermute(value, SHARD, pairs)  65.7 us
    ppermute x28, waiting for transfers between devices, shift(): return lax.ppermute(value, SHARD, pairs)  43 us
    unnamed x123, local copies, waits for them, and re-layouts  33.5 us
    reduce_scatter x4, waiting for transfers between devices, over_rep(): lax.psum_scatter(value.astype(low), CHIPS, scatter_dimension=0, tiled=True)  24 us
    dot_general x4, matrix products, mul_t(): lax.dot_general(left, right, (((1,), (1,)), ((), ())), preferred_element_...  15.7 us
  transfers between devices with their start and end apart: 55, of which 24 were waited for; matrix products, arithmetic and copies ran while one was open for 22% of the time, Pallas kernels for 0%

commit v1 on v0

--- a/solution.py
+++ b/solution.py
@@ -298,7 +298,12 @@
 
     def over_rep(value):
         owned = lax.psum_scatter(value.astype(low), CHIPS, scatter_dimension=0, tiled=True)
-        return core_join(lax.all_gather(owned, CHIPS, axis=0, tiled=True), core).astype(wide)
+        return core_join(
+            jnp.concatenate(
+                lax.all_to_all(jnp.stack([owned] * lax.axis_size(CHIPS)), CHIPS, 0, 0), axis=0
+            ),
+            core,
+        ).astype(wide)
 
     term_second = core_half(t_mul(active, grad_branch_second), core)
     grad_w_fc2 = over_rep(term_second)

time: 628 us -> 576 us (0.917)
  blocking collectives: 142 us -> 25.7 us
  waiting for transfers between devices: 148 us -> 200 us
  starting transfers between devices: 138 us -> 147 us
    all_gather x4 -> x0, blocking collectives: 142 us -> none  [over_rep(): lax.all_gather(owned, CHIPS, axis=0, tiled=True)]
    reduce_scatter x4, waiting for transfers between devices: 24 us -> 76.8 us  [over_rep(): lax.psum_scatter(value.astype(low), CHIPS, scatter_dimension=0, tiled=True)]
    all_to_all x0 -> x2, blocking collectives: none -> 25.7 us  [the longest x1 13.5 us: exchange(): return lax.all_to_all(value, axes, 0, 0, tiled=True)]
    all_to_all x15 -> x14, waiting for transfers between devices: 81.2 us -> 68.3 us  [exchange(): return lax.all_to_all(value, axes, 0, 0, tiled=True)]
    all_to_all x0 -> x3, waiting for transfers between devices: none -> 12.9 us  [over_rep(): lax.all_to_all(jnp.stack([owned] * lax.axis_size(CHIPS)), CHIPS, 0, 0)]
    all_to_all x0 -> x3, starting transfers between devices: none -> 10.5 us  [over_rep(): lax.all_to_all(jnp.stack([owned] * lax.axis_size(CHIPS)), CHIPS, 0, 0)]
    unnamed x123 -> x140, local copies, waits for them, and re-layouts: 33.5 us -> 30.7 us
    all_to_all x15 -> x14, starting transfers between devices: 71.2 us -> 72.5 us  [exchange(): return lax.all_to_all(value, axes, 0, 0, tiled=True)]
  transfers between devices with their start and end apart: 55 -> 57, of which waited for: 24 -> 26; matrix products, arithmetic and copies ran while one was open for 22% -> 27% of each run, Pallas kernels for 0% -> 0%
where the time goes in v1:
time: 576 us; the launch traced here: 569 us
  waiting for transfers between devices  200 us (35%)
  starting transfers between devices  147 us (26%)
  local copies, waits for them, and re-layouts  79.4 us (14%)
  matrix products  56.1 us (10%)
  other arithmetic  44.6 us (8%)
  blocking collectives  25.7 us (4%)
  between operations  15 us (3%)
    reduce_scatter x4, waiting for transfers between devices, over_rep(): lax.psum_scatter(value.astype(low), CHIPS, scatter_dimension=0, tiled=True)  76.8 us
    all_to_all x14, starting transfers between devices, exchange(): return lax.all_to_all(value, axes, 0, 0, tiled=True)  72.5 us
    all_to_all x14, waiting for transfers between devices, exchange(): return lax.all_to_all(value, axes, 0, 0, tiled=True)  68.3 us
    ppermute x28, starting transfers between devices, shift(): return lax.ppermute(value, SHARD, pairs)  63 us
    ppermute x28, waiting for transfers between devices, shift(): return lax.ppermute(value, SHARD, pairs)  40.8 us
    unnamed x140, local copies, waits for them, and re-layouts  30.7 us
    dot_general x4, matrix products, mul_t(): lax.dot_general(left, right, (((1,), (1,)), ((), ())), preferred_element_...  15.4 us
    all_to_all x1, blocking collectives, exchange(): return lax.all_to_all(value, axes, 0, 0, tiled=True)  13.5 us
  transfers between devices with their start and end apart: 57, of which 26 were waited for; matrix products, arithmetic and copies ran while one was open for 27% of the time, Pallas kernels for 0%

profile of v1, /device:TPU:0, one launch (start us, length us, event | category | flops | bytes accessed | tf_op | source)
XLA Modules:
  0.0 568.7 jit_solution(10711178031360224973)
XLA Ops:
  14.0 7.0 %all-to-all-start = ((f32[8,1,6656]{2,1,0:T(1,128)}), f32[8,1,6656]{2,1,0:T(1,128)S(1)}, u32[]{:S(2)}, u32[]{:S(2)}) async-start(f32[8,1,6656]{2,1,0:T(1,128)} %broadcast_in_dim.43), calls=%async_computation | async-start | bytes 425984 | tf_op jit(solution)/shard_map/all_to_all | solution.py:38
  23.5 6.0 %all-to-all-done = f32[8,1,6656]{2,1,0:T(1,128)S(1)} async-done(((f32[8,1,6656]{2,1,0:T(1,128)}), f32[8,1,6656]{2,1,0:T(1,128)S(1)}, u32[]{:S(2)}, u32[]{:S(2)}) %all-to-all-start) | async-done | bytes 213024 | tf_op jit(solution)/shard_map/all_to_all | solution.py:38
  33.1 5.6 collective-permute-start.19
  48.6 8.6 %all-to-all-start.1 = ((bf16[8,128,1024]{2,1,0:T(8,128)(2,1)}), bf16[8,128,1024]{2,1,0:T(8,128)(2,1)S(1)}, u32[]{:S(2)}, u32[]{:S(2)}) async-start(bf16[8,128,1024]{2,1,0:T(8,128)(2,1)} %broadcast_in_dim.45), calls=%async_computation.1 | async-start | bytes 4194304 | tf_op jit(solution)/shard_map/all_to_all | solution.py:38
  59.9 9.9 %collective-permute-done.14 = bf16[128,1024]{1,0:T(8,128)(2,1)} collective-permute-done((bf16[128,1024]{1,0:T(8,128)(2,1)}, bf16[128,1024]{1,0:T(8,128)(2,1)}, u32[]{:S(2)}, u32[]{:S(2)}) %collective-permute-start.14) | collective-permute-done | bytes 262176 | tf_op jit(solution)/shard_map/ppermute | solution.py:19
  69.8 8.2 %collective-permute-start.17 = (bf16[128,1024]{1,0:T(8,128)(2,1)}, bf16[128,1024]{1,0:T(8,128)(2,1)S(1)}, u32[]{:S(2)}, u32[]{:S(2)}) collective-permute-start(bf16[128,1024]{1,0:T(8,128)(2,1)} %bitcast.30), channel_id=1, source_target_pairs={{0,4},{1,5},{2,6},{3,7},{4,0},{5,1},{6,2},{7,3},{8,12},{9,13},{10,... | collective-permute-start | bytes 786440 | tf_op jit(solution)/shard_map/ppermute | solution.py:19
  109.7 10.5 %all-to-all-done.4 = bf16[8,128,1024]{2,1,0:T(8,128)(2,1)} async-done(((bf16[8,128,1024]{2,1,0:T(8,128)(2,1)}), bf16[8,128,1024]{2,1,0:T(8,128)(2,1)}, u32[]{:S(2)}, u32[]{:S(2)}) %all-to-all-start.4) | async-done | bytes 2097184 | tf_op jit(solution)/shard_map/all_to_all | solution.py:38
  120.2 4.7 all-to-all-start.3
  128.3 5.5 all-to-all-done.3
  146.3 6.5 %all-to-all-done.5 = bf16[8,128,512]{1,2,0:T(8,128)(2,1)} async-done(((bf16[8,128,512]{1,2,0:T(8,128)(2,1)}), bf16[8,128,512]{1,2,0:T(8,128)(2,1)}, u32[]{:S(2)}, u32[]{:S(2)}) %all-to-all-start.5) | async-done | bytes 1048608 | tf_op jit(solution)/shard_map/all_to_all | solution.py:38
  167.2 11.4 %collective-permute-done.1 = bf16[128,1024]{1,0:T(8,128)(2,1)S(1)} collective-permute-done((bf16[128,1024]{1,0:T(8,128)(2,1)}, bf16[128,1024]{1,0:T(8,128)(2,1)S(1)}, u32[]{:S(2)}, u32[]{:S(2)}) %collective-permute-start.1) | collective-permute-done | bytes 262176 | tf_op jit(solution)/shard_map/ppermute | solution.py:19
  178.6 5.5 collective-permute-start.4
  186.2 5.5 collective-permute-done.4
  201.4 4.9 collective-permute-start.13
  206.3 5.1 convert_reduce_fusion.3
  217.5 4.8 collective-permute-start.26
  276.6 5.9 %all-to-all-done.6 = bf16[8,128,128]{2,1,0:T(8,128)(2,1)} async-done(((bf16[8,128,128]{2,1,0:T(8,128)(2,1)}), bf16[8,128,128]{2,1,0:T(8,128)(2,1)}, u32[]{:S(2)}, u32[]{:S(2)}) %all-to-all-start.6) | async-done | bytes 262176 | tf_op jit(solution)/shard_map/all_to_all | solution.py:38
  283.8 5.1 fusion.16
  321.9 11.8 %all-to-all-done.16 = bf16[8,64,512]{2,1,0:T(8,128)(2,1)S(1)} async-done(((bf16[8,64,512]{2,1,0:T(8,128)(2,1)}), bf16[8,64,512]{2,1,0:T(8,128)(2,1)S(1)}, u32[]{:S(2)}, u32[]{:S(2)}) %all-to-all-start.16) | async-done | bytes 524320 | tf_op jit(solution)/shard_map/all_to_all | solution.py:38
  333.7 13.5 %all_to_all.109 = bf16[8,64,384]{2,1,0:T(8,128)(2,1)} all-to-all(bf16[8,64,384]{2,1,0:T(8,128)(2,1)S(1)} %fusion.55), channel_id=1, replica_groups=mesh['xl'=2,'z'=4,'core'=2,'xh'=2,'y'=4] {'xh','y'}, dimensions={0} | all-to-all | bytes 786432 | tf_op jit(solution)/shard_map/all_to_all | solution.py:38
  349.7 12.2 %all_to_all.110 = bf16[8,32,1024]{2,1,0:T(8,128)(2,1)} all-to-all(bf16[8,32,1024]{2,1,0:T(8,128)(2,1)S(1)} %stack.11), channel_id=1, replica_groups=mesh['xl'=2,'z'=4,'core'=2,'xh'=2,'y'=4] {'xl','z'}, dimensions={0} | all-to-all | bytes 1048576 | tf_op jit(solution)/shard_map/all_to_all | solution.py:303
  361.9 6.2 %all-to-all-start.7 = ((bf16[8,128,1024]{2,1,0:T(8,128)(2,1)}), bf16[8,128,1024]{2,1,0:T(8,128)(2,1)S(1)}, u32[]{:S(2)}, u32[]{:S(2)}) async-start(bf16[8,128,1024]{2,1,0:T(8,128)(2,1)} %bitcast.232), calls=%async_computation.7 | async-start | bytes 4194304 | tf_op jit(solution)/shard_map/all_to_all | solution.py:38
  379.6 10.5 %all-to-all-done.7 = bf16[8,128,1024]{2,1,0:T(8,128)(2,1)S(1)} async-done(((bf16[8,128,1024]{2,1,0:T(8,128)(2,1)}), bf16[8,128,1024]{2,1,0:T(8,128)(2,1)S(1)}, u32[]{:S(2)}, u32[]{:S(2)}) %all-to-all-start.7) | async-done | bytes 2097184 | tf_op jit(solution)/shard_map/all_to_all | solution.py:38
  397.7 15.2 %reduce-scatter.7.cloned.1.call-done = bf16[8,3072]{1,0:T(8,128)(2,1)} async-done(((bf16[64,3072]{1,0:T(8,128)(2,1)}), bf16[8,3072]{1,0:T(8,128)(2,1)}) %reduce-scatter.7.cloned.1.call-update) | async-done | bytes 49168 | tf_op jit(solution)/shard_map/reduce_scatter | solution.py:300
  419.0 33.5 %reduce-scatter.13.cloned.1.call-done = bf16[8,4096]{1,0:T(8,128)(2,1)} async-done(((bf16[64,4096]{1,0:T(8,128)(2,1)}), bf16[8,4096]{1,0:T(8,128)(2,1)}) %reduce-scatter.13.cloned.1.call-update) | async-done | bytes 65552 | tf_op jit(solution)/shard_map/reduce_scatter | solution.py:300
  457.9 8.2 %all-to-all-done.17 = bf16[8,8,4096]{2,1,0:T(8,128)(2,1)S(1)} async-done(((bf16[8,8,4096]{2,1,0:T(8,128)(2,1)}), bf16[8,8,4096]{2,1,0:T(8,128)(2,1)S(1)}, u32[]{:S(2)}, u32[]{:S(2)}) %all-to-all-start.17) | async-done | bytes 524320 | tf_op jit(solution)/shard_map/all_to_all | solution.py:303
  466.9 6.4 %all-to-all-start.8 = ((f32[8,1,7168]{2,1,0:T(1,128)}), f32[8,1,7168]{2,1,0:T(1,128)}, u32[]{:S(2)}, u32[]{:S(2)}) async-start(f32[8,1,7168]{2,1,0:T(1,128)} %broadcast_in_dim.49), calls=%async_computation.8 | async-start | bytes 458752 | tf_op jit(solution)/shard_map/all_to_all | solution.py:38
  484.1 5.4 all-to-all-start.9
  490.4 26.5 %reduce-scatter.9.cloned.1.call-done = bf16[8,1024]{1,0:T(8,128)(2,1)} async-done(((bf16[64,1024]{1,0:T(8,128)(2,1)}), bf16[8,1024]{1,0:T(8,128)(2,1)}) %reduce-scatter.9.cloned.1.call-update) | async-done | bytes 16400 | tf_op jit(solution)/shard_map/reduce_scatter | solution.py:300
  523.4 4.7 all-to-all-done.15
  537.8 5.2 all-to-all-done.12
  544.5 6.4 %all-to-all-start.13 = ((f32[8,1,256]{2,1,0:T(1,128)}), f32[8,1,256]{2,1,0:T(1,128)S(1)}, u32[]{:S(2)}, u32[]{:S(2)}) async-start(f32[8,1,256]{2,1,0:T(1,128)} %broadcast_in_dim.52), calls=%async_computation.14 | async-start | bytes 16384 | tf_op jit(solution)/shard_map/all_to_all | solution.py:38
  (356 shorter events, 267.4 us)
Async XLA Ops:
  33.1 93.5 %collective-permute-start.19 = (bf16[128,1024]{1,0:T(8,128)(2,1)}, bf16[128,1024]{1,0:T(8,128)(2,1)}, u32[]{:S(2)}, u32[]{:S(2)}) collective-permute-start(bf16[128,1024]{1,0:T(8,128)(2,1)} %bitcast.30), channel_id=1, source_target_pairs={{0,7},{1,4},{2,5},{3,6},{4,3},{5,0},{6,1},{7,2},{8,15},{9,12},{10,... | collective-permute-start | bytes 786440 | tf_op jit(solution)/shard_map/ppermute | solution.py:19
  38.6 86.3 %collective-permute-start.18 = (bf16[128,1024]{1,0:T(8,128)(2,1)}, bf16[128,1024]{1,0:T(8,128)(2,1)}, u32[]{:S(2)}, u32[]{:S(2)}) collective-permute-start(bf16[128,1024]{1,0:T(8,128)(2,1)} %bitcast.30), channel_id=1, source_target_pairs={{0,5},{1,6},{2,7},{3,4},{4,1},{5,2},{6,3},{7,0},{8,13},{9,14},{10,... | collective-permute-start | bytes 786440 | tf_op jit(solution)/shard_map/ppermute | solution.py:19
  38.6 42.8 %collective-permute-start.16 = (bf16[128,1024]{1,0:T(8,128)(2,1)}, bf16[128,1024]{1,0:T(8,128)(2,1)}, u32[]{:S(2)}, u32[]{:S(2)}) collective-permute-start(bf16[128,1024]{1,0:T(8,128)(2,1)} %bitcast.30), channel_id=1, source_target_pairs={{0,2},{1,3},{2,0},{3,1},{4,6},{5,7},{6,4},{7,5},{8,10},{9,11},{10,... | collective-permute-start | bytes 786440 | tf_op jit(solution)/shard_map/ppermute | solution.py:19
  40.9 38.8 %collective-permute-start.15 = (bf16[128,1024]{1,0:T(8,128)(2,1)}, bf16[128,1024]{1,0:T(8,128)(2,1)}, u32[]{:S(2)}, u32[]{:S(2)}) collective-permute-start(bf16[128,1024]{1,0:T(8,128)(2,1)} %bitcast.30), channel_id=1, source_target_pairs={{0,3},{1,0},{2,1},{3,2},{4,7},{5,4},{6,5},{7,6},{8,11},{9,8},{10,9... | collective-permute-start | bytes 786440 | tf_op jit(solution)/shard_map/ppermute | solution.py:19
  42.1 27.7 %collective-permute-start.14 = (bf16[128,1024]{1,0:T(8,128)(2,1)}, bf16[128,1024]{1,0:T(8,128)(2,1)}, u32[]{:S(2)}, u32[]{:S(2)}) collective-permute-start(bf16[128,1024]{1,0:T(8,128)(2,1)} %bitcast.30), channel_id=1, source_target_pairs={{0,1},{1,2},{2,3},{3,0},{4,5},{5,6},{6,7},{7,4},{8,9},{9,10},{10,1... | collective-permute-start | bytes 786440 | tf_op jit(solution)/shard_map/ppermute | solution.py:19
  48.6 41.7 %all-to-all-start.1 = ((bf16[8,128,1024]{2,1,0:T(8,128)(2,1)}), bf16[8,128,1024]{2,1,0:T(8,128)(2,1)S(1)}, u32[]{:S(2)}, u32[]{:S(2)}) async-start(bf16[8,128,1024]{2,1,0:T(8,128)(2,1)} %broadcast_in_dim.45), calls=%async_computation.1 | async-start | bytes 4194304 | tf_op jit(solution)/shard_map/all_to_all | solution.py:38
  79.7 64.9 %collective-permute-start.20 = (bf16[128,1024]{1,0:T(8,128)(2,1)}, bf16[128,1024]{1,0:T(8,128)(2,1)}, u32[]{:S(2)}, u32[]{:S(2)}) collective-permute-start(bf16[128,1024]{1,0:T(8,128)(2,1)} %bitcast.30), channel_id=1, source_target_pairs={{0,6},{1,7},{2,4},{3,5},{4,2},{5,3},{6,0},{7,1},{8,14},{9,15},{10,... | collective-permute-start | bytes 786440 | tf_op jit(solution)/shard_map/ppermute | solution.py:19
  92.7 27.4 %all-to-all-start.4 = ((bf16[8,128,1024]{2,1,0:T(8,128)(2,1)}), bf16[8,128,1024]{2,1,0:T(8,128)(2,1)}, u32[]{:S(2)}, u32[]{:S(2)}) async-start(bf16[8,128,1024]{2,1,0:T(8,128)(2,1)} %broadcast_in_dim.46), calls=%async_computation.4 | async-start | bytes 4194304 | tf_op jit(solution)/shard_map/all_to_all | solution.py:38
  133.8 19.0 %all-to-all-start.5 = ((bf16[8,128,512]{1,2,0:T(8,128)(2,1)}), bf16[8,128,512]{1,2,0:T(8,128)(2,1)}, u32[]{:S(2)}, u32[]{:S(2)}) async-start(bf16[8,128,512]{1,2,0:T(8,128)(2,1)} %bitcast.221), calls=%async_computation.5 | async-start | bytes 2097152 | tf_op jit(solution)/shard_map/all_to_all | solution.py:38
  142.8 21.7 %collective-permute-start = (bf16[128,1024]{1,0:T(8,128)(2,1)}, bf16[128,1024]{1,0:T(8,128)(2,1)}, u32[]{:S(2)}, u32[]{:S(2)}) collective-permute-start(bf16[128,1024]{1,0:T(8,128)(2,1)} %get-tuple-element.28), channel_id=1, source_target_pairs={{0,1},{1,2},{2,3},{3,0},{4,5},{5,6},{6,7},{7,4},{8,9},{9,10},{10,1... | collective-permute-start | bytes 786440 | tf_op jit(solution)/shard_map/ppermute | solution.py:19
  155.1 29.7 %collective-permute-start.2 = (bf16[128,1024]{1,0:T(8,128)(2,1)}, bf16[128,1024]{1,0:T(8,128)(2,1)S(1)}, u32[]{:S(2)}, u32[]{:S(2)}) collective-permute-start(bf16[128,1024]{1,0:T(8,128)(2,1)} %get-tuple-element.28), channel_id=1, source_target_pairs={{0,2},{1,3},{2,0},{3,1},{4,6},{5,7},{6,4},{7,5},{8,10},{9,11},{10,... | collective-permute-start | bytes 786440 | tf_op jit(solution)/shard_map/ppermute | solution.py:19
  157.2 21.4 %collective-permute-start.1 = (bf16[128,1024]{1,0:T(8,128)(2,1)}, bf16[128,1024]{1,0:T(8,128)(2,1)S(1)}, u32[]{:S(2)}, u32[]{:S(2)}) collective-permute-start(bf16[128,1024]{1,0:T(8,128)(2,1)} %get-tuple-element.28), channel_id=1, source_target_pairs={{0,3},{1,0},{2,1},{3,2},{4,7},{5,4},{6,5},{7,6},{8,11},{9,8},{10,9... | collective-permute-start | bytes 786440 | tf_op jit(solution)/shard_map/ppermute | solution.py:19
  158.5 34.7 %collective-permute-start.6 = (bf16[128,1024]{1,0:T(8,128)(2,1)}, bf16[128,1024]{1,0:T(8,128)(2,1)S(1)}, u32[]{:S(2)}, u32[]{:S(2)}) collective-permute-start(bf16[128,1024]{1,0:T(8,128)(2,1)} %get-tuple-element.28), channel_id=1, source_target_pairs={{0,6},{1,7},{2,4},{3,5},{4,2},{5,3},{6,0},{7,1},{8,14},{9,15},{10,... | collective-permute-start | bytes 786440 | tf_op jit(solution)/shard_map/ppermute | solution.py:19
  161.8 30.6 %collective-permute-start.5 = (bf16[128,1024]{1,0:T(8,128)(2,1)}, bf16[128,1024]{1,0:T(8,128)(2,1)S(1)}, u32[]{:S(2)}, u32[]{:S(2)}) collective-permute-start(bf16[128,1024]{1,0:T(8,128)(2,1)} %get-tuple-element.28), channel_id=1, source_target_pairs={{0,7},{1,4},{2,5},{3,6},{4,3},{5,0},{6,1},{7,2},{8,15},{9,12},{10,... | collective-permute-start | bytes 786440 | tf_op jit(solution)/shard_map/ppermute | solution.py:19
  164.4 21.1 %collective-permute-start.3 = (bf16[128,1024]{1,0:T(8,128)(2,1)}, bf16[128,1024]{1,0:T(8,128)(2,1)S(1)}, u32[]{:S(2)}, u32[]{:S(2)}) collective-permute-start(bf16[128,1024]{1,0:T(8,128)(2,1)} %get-tuple-element.28), channel_id=1, source_target_pairs={{0,4},{1,5},{2,6},{3,7},{4,0},{5,1},{6,2},{7,3},{8,12},{9,13},{10,... | collective-permute-start | bytes 786440 | tf_op jit(solution)/shard_map/ppermute | solution.py:19
  201.4 25.4 %collective-permute-start.7 = (bf16[128,1024]{1,0:T(8,128)(2,1)S(1)}, bf16[128,1024]{1,0:T(8,128)(2,1)S(1)}, u32[]{:S(2)}, u32[]{:S(2)}) collective-permute-start(bf16[128,1024]{1,0:T(8,128)(2,1)S(1)} %get-tuple-element.40), channel_id=1, source_target_pairs={{0,3},{1,0},{2,1},{3,2},{4,7},{5,4},{6,5},{7,6},{8,11},{9,8},{10,9... | collective-permute-start | bytes 786440 | tf_op jit(solution)/shard_map/ppermute | solution.py:19
  201.4 26.4 %collective-permute-start.13 = (bf16[128,1024]{1,0:T(8,128)(2,1)S(1)}, bf16[128,1024]{1,0:T(8,128)(2,1)S(1)}, u32[]{:S(2)}, u32[]{:S(2)}) collective-permute-start(bf16[128,1024]{1,0:T(8,128)(2,1)S(1)} %get-tuple-element.41), channel_id=1, source_target_pairs={{0,6},{1,7},{2,4},{3,5},{4,2},{5,3},{6,0},{7,1},{8,14},{9,15},{10,... | collective-permute-start | bytes 786440 | tf_op jit(solution)/shard_map/ppermute | solution.py:19
  217.5 23.6 %collective-permute-start.26 = (bf16[128,1024]{1,0:T(8,128)(2,1)}, bf16[128,1024]{1,0:T(8,128)(2,1)}, u32[]{:S(2)}, u32[]{:S(2)}) collective-permute-start(bf16[128,1024]{1,0:T(8,128)(2,1)} %get-tuple-element.35), channel_id=1, source_target_pairs={{0,5},{1,6},{2,7},{3,4},{4,1},{5,2},{6,3},{7,0},{8,13},{9,14},{10,... | collective-permute-start | bytes 786440 | tf_op jit(solution)/shard_map/ppermute | solution.py:19
  227.9 18.9 %collective-permute-start.24 = (bf16[128,1024]{1,0:T(8,128)(2,1)}, bf16[128,1024]{1,0:T(8,128)(2,1)}, u32[]{:S(2)}, u32[]{:S(2)}) collective-permute-start(bf16[128,1024]{1,0:T(8,128)(2,1)} %get-tuple-element.37), channel_id=1, source_target_pairs={{0,4},{1,5},{2,6},{3,7},{4,0},{5,1},{6,2},{7,3},{8,12},{9,13},{10,... | collective-permute-start | bytes 786440 | tf_op jit(solution)/shard_map/ppermute | solution.py:19
  254.4 55.1 %collective-permute-start.34 = (bf16[256,1024]{1,0:T(8,128)(2,1)}, bf16[256,1024]{1,0:T(8,128)(2,1)}, u32[]{:S(2)}, u32[]{:S(2)}) collective-permute-start(bf16[256,1024]{1,0:T(8,128)(2,1)} %dynamic-slice_convert_fusion.1), channel_id=1, source_target_pairs={{0,8},{8,0},{1,9},{9,1},{2,10},{10,2},{3,11},{11,3},{4,12},{12,4},... | collective-permute-start | bytes 1572872 | tf_op jit(solution)/shard_map/ppermute | solution.py:34
  273.3 75.5 %reduce-scatter.11.cloned.1.call-start = ((), (), s32[]{:S(2)}) async-start(), calls=%async_computation.25 | async-start | bytes 589824 | tf_op jit(solution)/shard_map/reduce_scatter | solution.py:300
  276.5 35.3 %collective-permute-start.32 = (bf16[64,4096]{1,0:T(8,128)(2,1)}, bf16[64,4096]{1,0:T(8,128)(2,1)}, u32[]{:S(2)}, u32[]{:S(2)}) collective-permute-start(bf16[64,4096]{1,0:T(8,128)(2,1)} %copy.215), channel_id=1, source_target_pairs={{0,8},{8,0},{1,9},{9,1},{2,10},{10,2},{3,11},{11,3},{4,12},{12,4},... | collective-permute-start | bytes 1572872 | tf_op jit(solution)/shard_map/ppermute | solution.py:34
  361.9 28.2 %all-to-all-start.7 = ((bf16[8,128,1024]{2,1,0:T(8,128)(2,1)}), bf16[8,128,1024]{2,1,0:T(8,128)(2,1)S(1)}, u32[]{:S(2)}, u32[]{:S(2)}) async-start(bf16[8,128,1024]{2,1,0:T(8,128)(2,1)} %bitcast.232), calls=%async_computation.7 | async-start | bytes 4194304 | tf_op jit(solution)/shard_map/all_to_all | solution.py:38
  368.2 44.8 %reduce-scatter.7.cloned.1.call-start = ((), (), s32[]{:S(2)}) async-start(), calls=%async_computation.23 | async-start | bytes 442368 | tf_op jit(solution)/shard_map/reduce_scatter | solution.py:300
  390.1 22.8 %all-to-all-start.14 = ((bf16[8,64,1024]{2,1,0:T(8,128)(2,1)}), bf16[8,64,1024]{2,1,0:T(8,128)(2,1)}, u32[]{:S(2)}, u32[]{:S(2)}) async-start(bf16[8,64,1024]{2,1,0:T(8,128)(2,1)} %fusion.24), calls=%async_computation.15 | async-start | bytes 2097152 | tf_op jit(solution)/shard_map/all_to_all | solution.py:38
  394.4 58.2 %reduce-scatter.13.cloned.1.call-start = ((), (), s32[]{:S(2)}) async-start(), calls=%async_computation.26 | async-start | bytes 589824 | tf_op jit(solution)/shard_map/reduce_scatter | solution.py:300
  414.5 38.0 %all-to-all-start.11 = ((bf16[8,8,3072]{2,1,0:T(8,128)(2,1)}), bf16[8,8,3072]{2,1,0:T(8,128)(2,1)S(1)}, u32[]{:S(2)}, u32[]{:S(2)}) async-start(bf16[8,8,3072]{2,1,0:T(8,128)(2,1)} %stack.8), calls=%async_computation.12 | async-start | bytes 786432 | tf_op jit(solution)/shard_map/all_to_all | solution.py:303
  473.3 43.6 %reduce-scatter.9.cloned.1.call-start = ((), (), s32[]{:S(2)}) async-start(), calls=%async_computation.24 | async-start | bytes 147456 | tf_op jit(solution)/shard_map/reduce_scatter | solution.py:300
  477.3 45.0 %collective-permute-start.35 = (bf16[256,1024]{1,0:T(8,128)(2,1)S(1)}, bf16[256,1024]{1,0:T(8,128)(2,1)}, u32[]{:S(2)}, u32[]{:S(2)}) collective-permute-start(bf16[256,1024]{1,0:T(8,128)(2,1)S(1)} %bitcast.228), channel_id=1, source_target_pairs={{0,8},{8,0},{1,9},{9,1},{2,10},{10,2},{3,11},{11,3},{4,12},{12,4},... | collective-permute-start | bytes 1572872 | tf_op jit(solution)/shard_map/ppermute | solution.py:34
  479.5 56.0 %collective-permute-start.29 = (bf16[64,3072]{1,0:T(8,128)(2,1)S(1)}, bf16[64,3072]{1,0:T(8,128)(2,1)}, u32[]{:S(2)}, u32[]{:S(2)}) collective-permute-start(bf16[64,3072]{1,0:T(8,128)(2,1)S(1)} %bitcast.240), channel_id=1, source_target_pairs={{0,8},{8,0},{1,9},{9,1},{2,10},{10,2},{3,11},{11,3},{4,12},{12,4},... | collective-permute-start | bytes 1179656 | tf_op jit(solution)/shard_map/ppermute | solution.py:34
  480.1 79.2 %collective-permute-start.33 = (bf16[64,4096]{1,0:T(8,128)(2,1)S(1)}, bf16[64,4096]{1,0:T(8,128)(2,1)}, u32[]{:S(2)}, u32[]{:S(2)}) collective-permute-start(bf16[64,4096]{1,0:T(8,128)(2,1)S(1)} %bitcast.229), channel_id=1, source_target_pairs={{0,8},{8,0},{1,9},{9,1},{2,10},{10,2},{3,11},{11,3},{4,12},{12,4},... | collective-permute-start | bytes 1572872 | tf_op jit(solution)/shard_map/ppermute | solution.py:34
  484.1 32.8 %all-to-all-start.9 = ((f32[8,1,128]{2,1,0:T(1,128)}), f32[8,1,128]{2,1,0:T(1,128)S(1)}, u32[]{:S(2)}, u32[]{:S(2)}) async-start(f32[8,1,128]{2,1,0:T(1,128)} %broadcast_in_dim.50), calls=%async_computation.9 | async-start | bytes 8192 | tf_op jit(solution)/shard_map/all_to_all | solution.py:38
  (78 other events, 1129.8 us)
Sparse Core Ops, SparseCore 0:
  311.9 36.8 reduce-scatter.10
  374.9 37.9 reduce-scatter.6
  415.9 36.6 reduce-scatter.12
  479.6 37.2 reduce-scatter.8
